TPU v7x, 256 devices: a whole 4x4x8 slice. The times are simulated.
256 devices in a mesh: req: 32 (over y, z), head: 2 (over core), grp: 4 (over x).
Axes of the slice: x: 4, y: 4, z: 8, core: 2. Of those that a mesh axis runs over, the one named last changes fastest.
Arguments:
- residual: bfloat16 [1024, 7168], P(('req', 'grp'), 'head'), may hold values from -12 to 12
- attn_part: bfloat16 [2, 1024, 7168], P('head', ('req', 'grp')), may hold values from -6 to 6
- norm_gain: float32 [7168], P('head'), may hold values from 0.1 to 1.9
- routes: int32 [1024, 8], P(('req', 'grp')), may hold values from 0 to 31, all different within a row; in each aligned block of 8 rows (0 to 7, 8 to 15, ...) at most 4 rows name the same one
- gates: float32 [1024, 8], P(('req', 'grp')), may hold values from 0.1 to 0.6
- gate_weight: bfloat16 [32, 7168, 2048], P('req', None, ('head', 'grp')), may hold values from -0.0625 to 0.0625
- up_weight: bfloat16 [32, 7168, 2048], P('req', None, ('head', 'grp')), may hold values from -0.0625 to 0.0625
- down_weight: bfloat16 [32, 2048, 7168], P('req', None, ('head', 'grp')), may hold values from -0.125 to 0.125
Outputs:
- mixed: bfloat16 [1024, 7168], P(('req', 'grp'), 'head')
Inputs may be any that keep to these rules, and one draw needn't show every extreme that they name: `routes`: each row names 8 different experts. In each aligned block of 8 rows (the rows of one index pair of req and grp) no expert is named more than 4 times, a bound that some block reaches.
All inputs are finite; a program needn't handle non-finite values.
Results may differ from a plain program's by a relative error of at most 0.012.
Values may be sent and summed in bfloat16 or wider, within the bound.
A program may use at most 128 MiB of HBM per device.

v0:
```python
import jax
import jax.numpy as jnp
from jax import lax
from jax.sharding import PartitionSpec as P

D = 7168
CAP = 4
EPSILON = 1e-06


def slot_places(routes, experts):
    count_rows, count_top = routes.shape
    flat_routes = routes.reshape(count_rows * count_top)
    onehot = (flat_routes[:, None] == jnp.arange(experts, dtype=jnp.int32)[None, :]).astype(
        jnp.int32
    )
    earlier = jnp.cumsum(onehot, axis=0) - onehot
    slot_index = jnp.sum(earlier * onehot, axis=1).reshape(count_rows, count_top)
    return routes * CAP + slot_index


def select_table(places, experts):
    return places[:, :, None] == jnp.arange(experts * CAP, dtype=jnp.int32)[None, None, :]


def expert_hidden(arrived, gate_weight, up_weight):
    groups, sources, columns, features = arrived.shape
    local_experts = gate_weight.shape[0]
    shaped = arrived.reshape(groups, sources, local_experts, columns // local_experts, features)
    gate_act = jnp.einsum(
        "gresd,edf->gresf", shaped, gate_weight, preferred_element_type=jnp.float32
    )
    up_act = jnp.einsum("gresd,edf->gresf", shaped, up_weight, preferred_element_type=jnp.float32)
    return (jax.nn.silu(gate_act) * up_act).astype(jnp.bfloat16)


def on_device(residual, attn_part, norm_gain, routes, gates, gate_weight, up_weight, down_weight):
    req_count = lax.axis_size("req")
    experts = gate_weight.shape[0] * req_count
    summed = lax.psum_scatter(
        attn_part[0].astype(jnp.float32).astype(jnp.bfloat16),
        "head",
        scatter_dimension=1,
        tiled=True,
    ).astype(jnp.float32)
    hidden_state = residual.astype(jnp.float32) + summed
    squares = lax.psum(jnp.sum(hidden_state * hidden_state, axis=1), "head")
    row_scale = lax.rsqrt(squares / D + EPSILON)
    normed = (hidden_state * row_scale[:, None] * norm_gain[None, :]).astype(jnp.bfloat16)
    selected = select_table(slot_places(routes, experts), experts)
    weighting = jnp.sum(jnp.where(selected, gates[:, :, None], 0.0), axis=1)
    packing = jnp.any(selected, axis=1).astype(jnp.bfloat16)
    packed = jnp.einsum("tj,td->jd", packing, normed, preferred_element_type=jnp.float32).astype(
        jnp.bfloat16
    )
    packed = packed.reshape(req_count, -1, normed.shape[1])
    arrived = lax.all_to_all(packed, "req", split_axis=0, concat_axis=0, tiled=True)
    whole_rows = lax.all_gather(arrived, "head", axis=2, tiled=True)
    hidden_units = expert_hidden(
        lax.all_gather(whole_rows[None], "grp", axis=0, tiled=True), gate_weight, up_weight
    )
    projected = jnp.einsum(
        "gresf,efd->gresd",
        lax.all_gather(hidden_units, ("head", "grp"), axis=4, tiled=True),
        down_weight,
        preferred_element_type=jnp.float32,
    )
    outgoing = projected.astype(jnp.bfloat16)
    regrouped = lax.all_to_all(outgoing, "grp", split_axis=0, concat_axis=4, tiled=True)
    regrouped = regrouped.reshape(req_count, -1, regrouped.shape[4])
    returned = lax.all_to_all(regrouped, "req", split_axis=0, concat_axis=0, tiled=True)
    back_rows = returned.reshape(-1, returned.shape[-1]).astype(jnp.float32)
    routed = jnp.dot(weighting, back_rows, precision=lax.Precision.HIGHEST)
    return (hidden_state + routed).astype(jnp.bfloat16)


def solution(mesh):
    placed = (
        P(("req", "grp"), "head"),
        P("head", ("req", "grp"), None),
        P("head"),
        P(("req", "grp"), None),
        P(("req", "grp"), None),
        P("req", None, ("head", "grp")),
        P("req", None, ("head", "grp")),
        P("req", None, ("head", "grp")),
    )
    return jax.shard_map(
        on_device, mesh=mesh, in_specs=placed, out_specs=P(("req", "grp"), "head"), check_vma=False
    )
```

profile of v0, /device:TPU:32, one launch (start us, length us, event | category | flops | bytes accessed | tf_op | source)
XLA Modules:
  0.0 268.5 jit_solution(15193154326299129199)
XLA Ops:
  6.5 0.7 reduce-scatter.2.cloned.1.call-update
  7.3 0.8 eq.28
  8.5 0.7 multiply_add_fusion
  9.2 16.0 %reduce-scatter.2.cloned.1.call-done = bf16[8,3584]{1,0:T(8,128)(2,1)} async-done(((bf16[8,7168]{1,0:T(8,128)(2,1)}), bf16[8,3584]{1,0:T(8,128)(2,1)}) %reduce-scatter.2.cloned.1.call-update) | async-done | bytes 57360 | tf_op jit(solution)/shard_map/reduce_scatter | solution.py:40
  25.3 1.0 multiply_reduce_fusion
  26.3 2.5 psum.7
  28.8 1.3 convolution_convert_fusion
  30.1 0.2 reshape.40
  30.4 36.0 %all_to_all.25 = bf16[32,4,3584]{2,1,0:T(4,128)(2,1)S(1)} all-to-all(bf16[32,4,3584]{2,1,0:T(4,128)(2,1)S(1)} %reshape.40), channel_id=1, replica_groups=mesh['req'=32,'head'=2,'grp'=4] {'req'}, dimensions={0} | all-to-all | bytes 1835008 | tf_op jit(solution)/shard_map/all_to_all | solution.py:57
  66.3 1.1 copy.24
  67.5 12.1 %all-gather.5.cloned.1.call-done = bf16[32,4,7168]{2,0,1:T(8,128)(2,1)} async-done(((bf16[32,4,3584]{2,0,1:T(8,128)(2,1)}), bf16[32,4,7168]{2,0,1:T(8,128)(2,1)}) %all-gather.5.cloned.1.call-update) | async-done | bytes 1835024 | tf_op jit(solution)/shard_map/all_gather | solution.py:58
  79.7 80.0 %all-gather.9.cloned.1.call-done = bf16[128,4,7168]{2,0,1:T(8,128)(2,1)} async-done(((bf16[32,4,7168]{2,0,1:T(8,128)(2,1)}), bf16[128,4,7168]{2,0,1:T(8,128)(2,1)}) %all-gather.9.cloned.1.call-update) | async-done | bytes 7340048 | tf_op jit(solution)/shard_map/all_gather | solution.py:60
  159.7 6.3 %fusion.20 = f32[4,32,1,4,256]{4,1,3,0,2:T(8,128)S(1)} fusion(bf16[1,7168,256]{2,1,0:T(8,128)(2,1)} %param.13, bf16[4,32,4,7168]{3,1,0,2:T(8,128)(2,1)} %bitcast.76), kind=kOutput, calls=%fused_computation.14 | convolution fusion | flops 1879048192 | bytes 11534336 | tf_op jit(solution)/shard_map/gresd,edf->gresf/dot_general | solution.py:30
  166.0 0.9 copy-done.4
  166.9 2.8 %fusion.35 = bf16[4,32,1,4,256]{4,1,3,0,2:T(8,128)(2,1)} fusion(bf16[1,7168,256]{2,1,0:T(8,128)(2,1)S(1)} %copy-done.4, bf16[4,32,4,7168]{3,1,0,2:T(8,128)(2,1)S(1)} %bitcast.77, f32[4,32,1,4,256]{4,1,3,0,2:T(8,128)S(1)} %fusion.20), kind=kOutput, calls=%fused_computation.17 | convolution fusion | flops 1879834624 | bytes 11796480 | tf_op jit(solution)/shard_map/gresd,edf->gresf/dot_general | solution.py:33
  169.7 30.8 %all-gather.7.cloned.1.call-done = bf16[4,32,1,4,2048]{4,1,3,0,2:T(8,128)(2,1)} async-done(((bf16[4,32,1,4,256]{4,1,3,0,2:T(8,128)(2,1)}), bf16[4,32,1,4,2048]{4,1,3,0,2:T(8,128)(2,1)}) %all-gather.7.cloned.1.call-update) | async-done | bytes 2097168 | tf_op jit(solution)/shard_map/all_gather | solution.py:64
  200.5 5.0 %fusion.15 = bf16[4,32,1,4,896]{4,1,3,2,0:T(8,128)(2,1)S(1)} fusion(bf16[1,2048,896]{2,1,0:T(8,128)(2,1)} %param.15, bf16[4,32,1,4,2048]{4,1,3,0,2:T(8,128)(2,1)} %all-gather.7.cloned.1.call-done), kind=kOutput, calls=%fused_computation.13 | convolution fusion | flops 1879506944 | bytes 6684672 | tf_op jit(solution)/shard_map/gresf,efd->gresd/dot_general | solution.py:62
  205.6 17.9 %all_to_all.26 = bf16[4,32,1,4,896]{4,1,3,2,0:T(8,128)(2,1)S(1)} all-to-all(bf16[4,32,1,4,896]{4,1,3,2,0:T(8,128)(2,1)S(1)} %fusion.15), channel_id=1, replica_groups=mesh['req'=32,'head'=2,'grp'=4] {'grp'}, dimensions={0} | all-to-all | bytes 1835008 | tf_op jit(solution)/shard_map/all_to_all | solution.py:69
  223.4 0.7 copy.33
  224.2 1.3 reshape.51
  225.4 10.1 %all-to-all-start.2 = ((bf16[32,4,3584]{2,1,0:T(4,128)(2,1)}), bf16[32,4,3584]{2,1,0:T(4,128)(2,1)S(1)}, u32[]{:S(2)}, u32[]{:S(2)}) async-start(bf16[32,4,3584]{2,1,0:T(4,128)(2,1)} %reshape.51), calls=%async_computation.3 | async-start | bytes 1835008 | tf_op jit(solution)/shard_map/all_to_all | solution.py:71
  235.6 25.0 %all-to-all-done.2 = bf16[32,4,3584]{2,1,0:T(4,128)(2,1)S(1)} async-done(((bf16[32,4,3584]{2,1,0:T(4,128)(2,1)}), bf16[32,4,3584]{2,1,0:T(4,128)(2,1)S(1)}, u32[]{:S(2)}, u32[]{:S(2)}) %all-to-all-start.2) | async-done | bytes 917536 | tf_op jit(solution)/shard_map/all_to_all | solution.py:71
  260.6 0.2 reshape.46
  260.9 1.1 fusion.4
  (23 shorter events, 0.8 us)
Async XLA Ops:
  6.5 18.7 %reduce-scatter.2.cloned.1.call-start = ((), (), s32[]{:S(2)}) async-start(), calls=%async_computation.4 | async-start | bytes 172032 | tf_op jit(solution)/shard_map/reduce_scatter | solution.py:40
  7.3 72.4 %all-gather.5.cloned.1.call-start = ((), (), s32[]{:S(2)}) async-start(), calls=%async_computation.5 | async-start | bytes 2752512 | tf_op jit(solution)/shard_map/all_gather | solution.py:58
  67.4 92.2 %all-gather.9.cloned.1.call-start = ((), (), s32[]{:S(2)}) async-start(), calls=%async_computation.7 | async-start | bytes 9175040 | tf_op jit(solution)/shard_map/all_gather | solution.py:60
  79.6 120.9 %all-gather.7.cloned.1.call-start = ((), (), s32[]{:S(2)}) async-start(), calls=%async_computation.6 | async-start | bytes 2359296 | tf_op jit(solution)/shard_map/all_gather | solution.py:64
  159.7 6.3 %copy-start.3 = (bf16[128,4,7168]{2,0,1:T(8,128)(2,1)S(1)}, bf16[128,4,7168]{2,0,1:T(8,128)(2,1)}, u32[]{:S(2)}) copy-start(bf16[128,4,7168]{2,0,1:T(8,128)(2,1)} %all-gather.9.cloned.1.call-done) | copy-start | bytes 22020100
  159.7 7.3 %copy-start.4 = (bf16[1,7168,256]{2,1,0:T(8,128)(2,1)S(1)}, bf16[1,7168,256]{2,1,0:T(8,128)(2,1)}, u32[]{:S(2)}) copy-start(bf16[1,7168,256]{2,1,0:T(8,128)(2,1)} %param.14) | copy-start | bytes 11010052
  205.5 30.0 %copy-start.2 = (f32[8,8]{1,0:T(8,128)S(1)}, f32[8,8]{1,0:T(8,128)}, u32[]{:S(2)}) copy-start(f32[8,8]{1,0:T(8,128)} %param.12) | copy-start | bytes 772
  223.4 37.4 %copy-start = (bf16[8,3584]{1,0:T(8,128)(2,1)S(1)}, bf16[8,3584]{1,0:T(8,128)(2,1)}, u32[]{:S(2)}) copy-start(bf16[8,3584]{1,0:T(8,128)(2,1)} %param.8) | copy-start | bytes 172036
  223.4 37.4 %copy-start.1 = (bf16[8,3584]{1,0:T(8,128)(2,1)S(1)}, bf16[8,3584]{1,0:T(8,128)(2,1)}, u32[]{:S(2)}) copy-start(bf16[8,3584]{1,0:T(8,128)(2,1)} %reduce-scatter.2.cloned.1.call-done) | copy-start | bytes 172036
  225.4 35.2 %all-to-all-start.2 = ((bf16[32,4,3584]{2,1,0:T(4,128)(2,1)}), bf16[32,4,3584]{2,1,0:T(4,128)(2,1)S(1)}, u32[]{:S(2)}, u32[]{:S(2)}) async-start(bf16[32,4,3584]{2,1,0:T(4,128)(2,1)} %reshape.51), calls=%async_computation.3 | async-start | bytes 1835008 | tf_op jit(solution)/shard_map/all_to_all | solution.py:71
Sparse Core Ops, SparseCore 0:
  9.8 15.4 reduce-scatter.1
  67.5 12.0 all-gather.4
  81.4 78.1 all-gather.8
  169.8 30.6 all-gather.6
where the time goes:
time: 269 us
  waiting for transfers between devices  165 us (61%)
  blocking collectives  56.3 us (21%)
  matrix products  16.5 us (6%)
  between operations  13.2 us (5%)
  starting transfers between devices  10.2 us (4%)
  local copies, waits for them, and re-layouts  5.25 us (2%)
    all_gather x1, waiting for transfers between devices, on_device(): lax.all_gather(whole_rows[None], 'grp', axis=0, tiled=True)  80 us
    all_to_all x1, blocking collectives, on_device(): lax.all_to_all(packed, 'req', split_axis=0, concat_axis=0, tiled=True)  36 us
    all_gather x1, waiting for transfers between devices, on_device(): lax.all_gather(hidden_units, ('head', 'grp'), axis=4, tiled=True)  30.8 us
    all_to_all x1, waiting for transfers between devices, on_device(): lax.all_to_all(regrouped, 'req', split_axis=0, concat_axis=0, tiled=True)  25 us
    all_to_all x1, blocking collectives, on_device(): lax.all_to_all(outgoing, 'grp', split_axis=0, concat_axis=4, tiled=True)  17.9 us
    reduce_scatter x1, waiting for transfers between devices, on_device(): lax.psum_scatter(attn_part[0].astype(jnp.float32).astype(jnp.bfloat16), '...  16 us
    all_gather x1, waiting for transfers between devices, on_device(): whole_rows = lax.all_gather(arrived, 'head', axis=2, tiled=True)  12.1 us
    all_to_all x1, starting transfers between devices, on_device(): lax.all_to_all(regrouped, 'req', split_axis=0, concat_axis=0, tiled=True)  10.1 us
  transfers between devices with their start and end apart: 5, of which 5 were waited for; matrix products, arithmetic and copies ran while one was open for 1% of the time, Pallas kernels for 0%

commit v1 on v0

--- a/solution.py
+++ b/solution.py
@@ -66,7 +66,10 @@
         preferred_element_type=jnp.float32,
     )
     outgoing = projected.astype(jnp.bfloat16)
-    regrouped = lax.all_to_all(outgoing, "grp", split_axis=0, concat_axis=4, tiled=True)
+    regrouped = jnp.concatenate(
+        lax.all_to_all(jnp.stack(jnp.split(outgoing, lax.axis_size("grp"), axis=0)), "grp", 0, 0),
+        axis=4,
+    )
     regrouped = regrouped.reshape(req_count, -1, regrouped.shape[4])
     returned = lax.all_to_all(regrouped, "req", split_axis=0, concat_axis=0, tiled=True)
     back_rows = returned.reshape(-1, returned.shape[-1]).astype(jnp.float32)

time: 269 us -> 269 us (level)
  no operation moved by 1% of the time
where the time goes in v1:
time: 269 us
  waiting for transfers between devices  165 us (61%)
  blocking collectives  56.3 us (21%)
  matrix products  16.5 us (6%)
  between operations  13.3 us (5%)
  starting transfers between devices  10.2 us (4%)
  local copies, waits for them, and re-layouts  5.33 us (2%)
    all_gather x1, waiting for transfers between devices, on_device(): lax.all_gather(whole_rows[None], 'grp', axis=0, tiled=True)  80 us
    all_to_all x1, blocking collectives, on_device(): lax.all_to_all(packed, 'req', split_axis=0, concat_axis=0, tiled=True)  36 us
    all_gather x1, waiting for transfers between devices, on_device(): lax.all_gather(hidden_units, ('head', 'grp'), axis=4, tiled=True)  30.8 us
    all_to_all x1, waiting for transfers between devices, on_device(): lax.all_to_all(regrouped, 'req', split_axis=0, concat_axis=0, tiled=True)  25 us
    all_to_all x1, blocking collectives, on_device(): lax.all_to_all(jnp.stack(jnp.split(outgoing, lax.axis_size('grp'), axis=0...  17.9 us
    reduce_scatter x1, waiting for transfers between devices, on_device(): lax.psum_scatter(attn_part[0].astype(jnp.float32).astype(jnp.bfloat16), '...  16 us
    all_gather x1, waiting for transfers between devices, on_device(): whole_rows = lax.all_gather(arrived, 'head', axis=2, tiled=True)  12.1 us
    all_to_all x1, starting transfers between devices, on_device(): lax.all_to_all(regrouped, 'req', split_axis=0, concat_axis=0, tiled=True)  10.1 us
  transfers between devices with their start and end apart: 5, of which 5 were waited for; matrix products, arithmetic and copies ran while one was open for 1% of the time, Pallas kernels for 0%

profile of v1, /device:TPU:32, one launch (start us, length us, event | category | flops | bytes accessed | tf_op | source)
XLA Modules:
  0.0 268.8 jit_solution(16088205857763593847)
XLA Ops:
  6.5 0.7 reduce-scatter.2.cloned.1.call-update
  7.3 0.8 eq.28
  8.5 0.7 multiply_add_fusion
  9.2 16.0 %reduce-scatter.2.cloned.1.call-done = bf16[8,3584]{1,0:T(8,128)(2,1)} async-done(((bf16[8,7168]{1,0:T(8,128)(2,1)}), bf16[8,3584]{1,0:T(8,128)(2,1)}) %reduce-scatter.2.cloned.1.call-update) | async-done | bytes 57360 | tf_op jit(solution)/shard_map/reduce_scatter | solution.py:40
  25.3 1.0 multiply_reduce_fusion
  26.3 2.5 psum.7
  28.8 1.3 convolution_convert_fusion
  30.1 0.2 reshape.39
  30.4 36.0 %all_to_all.15 = bf16[32,4,3584]{2,1,0:T(4,128)(2,1)S(1)} all-to-all(bf16[32,4,3584]{2,1,0:T(4,128)(2,1)S(1)} %reshape.39), channel_id=1, replica_groups=mesh['req'=32,'head'=2,'grp'=4] {'req'}, dimensions={0} | all-to-all | bytes 1835008 | tf_op jit(solution)/shard_map/all_to_all | solution.py:57
  66.3 1.1 copy.35
  67.5 12.1 %all-gather.5.cloned.1.call-done = bf16[32,4,7168]{2,0,1:T(8,128)(2,1)} async-done(((bf16[32,4,3584]{2,0,1:T(8,128)(2,1)}), bf16[32,4,7168]{2,0,1:T(8,128)(2,1)}) %all-gather.5.cloned.1.call-update) | async-done | bytes 1835024 | tf_op jit(solution)/shard_map/all_gather | solution.py:58
  79.7 80.0 %all-gather.9.cloned.1.call-done = bf16[128,4,7168]{2,0,1:T(8,128)(2,1)} async-done(((bf16[32,4,7168]{2,0,1:T(8,128)(2,1)}), bf16[128,4,7168]{2,0,1:T(8,128)(2,1)}) %all-gather.9.cloned.1.call-update) | async-done | bytes 7340048 | tf_op jit(solution)/shard_map/all_gather | solution.py:60
  159.7 6.3 %fusion.15 = f32[4,32,1,4,256]{4,1,3,0,2:T(8,128)S(1)} fusion(bf16[1,7168,256]{2,1,0:T(8,128)(2,1)} %param.13, bf16[4,32,4,7168]{3,1,0,2:T(8,128)(2,1)} %bitcast.81), kind=kOutput, calls=%fused_computation.13 | convolution fusion | flops 1879048192 | bytes 11534336 | tf_op jit(solution)/shard_map/gresd,edf->gresf/dot_general | solution.py:30
  166.0 0.9 copy-done.4
  166.9 2.8 %fusion.30 = bf16[4,32,1,4,256]{4,1,3,0,2:T(8,128)(2,1)} fusion(bf16[1,7168,256]{2,1,0:T(8,128)(2,1)S(1)} %copy-done.4, bf16[4,32,4,7168]{3,1,0,2:T(8,128)(2,1)S(1)} %bitcast.82, f32[4,32,1,4,256]{4,1,3,0,2:T(8,128)S(1)} %fusion.15), kind=kOutput, calls=%fused_computation.16 | convolution fusion | flops 1879834624 | bytes 11796480 | tf_op jit(solution)/shard_map/gresd,edf->gresf/dot_general | solution.py:33
  169.7 30.8 %all-gather.7.cloned.1.call-done = bf16[4,32,1,4,2048]{4,1,3,0,2:T(8,128)(2,1)} async-done(((bf16[4,32,1,4,256]{4,1,3,0,2:T(8,128)(2,1)}), bf16[4,32,1,4,2048]{4,1,3,0,2:T(8,128)(2,1)}) %all-gather.7.cloned.1.call-update) | async-done | bytes 2097168 | tf_op jit(solution)/shard_map/all_gather | solution.py:64
  200.5 5.0 %fusion.10 = bf16[4,32,4,896]{3,1,2,0:T(8,128)(2,1)S(1)} fusion(bf16[1,2048,896]{2,1,0:T(8,128)(2,1)} %param.15, bf16[4,32,1,4,2048]{4,1,3,0,2:T(8,128)(2,1)} %all-gather.7.cloned.1.call-done), kind=kOutput, calls=%fused_computation.12 | convolution fusion | flops 1879506944 | bytes 6684672 | tf_op jit(solution)/shard_map/gresf,efd->gresd/dot_general | solution.py:62
  205.8 17.9 %all_to_all.16 = bf16[4,1,32,1,4,896]{5,2,4,3,1,0:T(8,128)(2,1)S(1)} all-to-all(bf16[4,1,32,1,4,896]{5,2,4,3,1,0:T(8,128)(2,1)S(1)} %pad_maximum_fusion), channel_id=1, replica_groups=mesh['req'=32,'head'=2,'grp'=4] {'grp'}, dimensions={0} | all-to-all | bytes 1835008 | tf_op jit(solution)/shard_map/all_to_all | solution.py:70
  223.7 0.7 copy.46
  224.4 1.3 reshape.50
  225.7 10.1 %all-to-all-start.2 = ((bf16[32,4,3584]{2,1,0:T(4,128)(2,1)}), bf16[32,4,3584]{2,1,0:T(4,128)(2,1)S(1)}, u32[]{:S(2)}, u32[]{:S(2)}) async-start(bf16[32,4,3584]{2,1,0:T(4,128)(2,1)} %reshape.50), calls=%async_computation.3 | async-start | bytes 1835008 | tf_op jit(solution)/shard_map/all_to_all | solution.py:74
  235.9 25.0 %all-to-all-done.2 = bf16[32,4,3584]{2,1,0:T(4,128)(2,1)S(1)} async-done(((bf16[32,4,3584]{2,1,0:T(4,128)(2,1)}), bf16[32,4,3584]{2,1,0:T(4,128)(2,1)S(1)}, u32[]{:S(2)}, u32[]{:S(2)}) %all-to-all-start.2) | async-done | bytes 917536 | tf_op jit(solution)/shard_map/all_to_all | solution.py:74
  260.9 0.2 reshape.45
  261.1 1.1 fusion.4
  (26 shorter events, 1.0 us)
Async XLA Ops:
  6.5 18.7 %reduce-scatter.2.cloned.1.call-start = ((), (), s32[]{:S(2)}) async-start(), calls=%async_computation.4 | async-start | bytes 172032 | tf_op jit(solution)/shard_map/reduce_scatter | solution.py:40
  7.3 72.4 %all-gather.5.cloned.1.call-start = ((), (), s32[]{:S(2)}) async-start(), calls=%async_computation.5 | async-start | bytes 2752512 | tf_op jit(solution)/shard_map/all_gather | solution.py:58
  67.4 92.2 %all-gather.9.cloned.1.call-start = ((), (), s32[]{:S(2)}) async-start(), calls=%async_computation.7 | async-start | bytes 9175040 | tf_op jit(solution)/shard_map/all_gather | solution.py:60
  79.6 120.9 %all-gather.7.cloned.1.call-start = ((), (), s32[]{:S(2)}) async-start(), calls=%async_computation.6 | async-start | bytes 2359296 | tf_op jit(solution)/shard_map/all_gather | solution.py:64
  159.7 6.3 %copy-start.3 = (bf16[128,4,7168]{2,0,1:T(8,128)(2,1)S(1)}, bf16[128,4,7168]{2,0,1:T(8,128)(2,1)}, u32[]{:S(2)}) copy-start(bf16[128,4,7168]{2,0,1:T(8,128)(2,1)} %all-gather.9.cloned.1.call-done) | copy-start | bytes 22020100
  159.7 7.3 %copy-start.4 = (bf16[1,7168,256]{2,1,0:T(8,128)(2,1)S(1)}, bf16[1,7168,256]{2,1,0:T(8,128)(2,1)}, u32[]{:S(2)}) copy-start(bf16[1,7168,256]{2,1,0:T(8,128)(2,1)} %param.14) | copy-start | bytes 11010052
  205.8 30.0 %copy-start.2 = (f32[8,8]{1,0:T(8,128)S(1)}, f32[8,8]{1,0:T(8,128)}, u32[]{:S(2)}) copy-start(f32[8,8]{1,0:T(8,128)} %param.12) | copy-start | bytes 772
  223.7 37.4 %copy-start = (bf16[8,3584]{1,0:T(8,128)(2,1)S(1)}, bf16[8,3584]{1,0:T(8,128)(2,1)}, u32[]{:S(2)}) copy-start(bf16[8,3584]{1,0:T(8,128)(2,1)} %param.8) | copy-start | bytes 172036
  223.7 37.4 %copy-start.1 = (bf16[8,3584]{1,0:T(8,128)(2,1)S(1)}, bf16[8,3584]{1,0:T(8,128)(2,1)}, u32[]{:S(2)}) copy-start(bf16[8,3584]{1,0:T(8,128)(2,1)} %reduce-scatter.2.cloned.1.call-done) | copy-start | bytes 172036
  225.7 35.2 %all-to-all-start.2 = ((bf16[32,4,3584]{2,1,0:T(4,128)(2,1)}), bf16[32,4,3584]{2,1,0:T(4,128)(2,1)S(1)}, u32[]{:S(2)}, u32[]{:S(2)}) async-start(bf16[32,4,3584]{2,1,0:T(4,128)(2,1)} %reshape.50), calls=%async_computation.3 | async-start | bytes 1835008 | tf_op jit(solution)/shard_map/all_to_all | solution.py:74
Sparse Core Ops, SparseCore 0:
  9.8 15.4 reduce-scatter.1
  67.5 12.0 all-gather.4
  81.4 78.1 all-gather.8
  169.8 30.6 all-gather.6
